TPU v7x, 32 devices: a whole 2x2x4 slice. The times are simulated.
32 devices in a mesh: ch: 8 (over z, x), tok: 4 (over y, core).
Axes of the slice: x: 2, y: 2, z: 4, core: 2. Of those that a mesh axis runs over, the one named last changes fastest.
Arguments:
- inputs: bfloat16 [4, 768, 4096], P(None, 'ch', 'tok'), may hold values from -6 to 6
- out_grad: bfloat16 [4, 768, 4096], P(None, 'ch', 'tok'), may hold values from -6 to 6
- seq_lengths: int32 [4], replicated, may hold values from 2560 to 4096, as said below
- ema_alpha: float32 [768, 16], P('ch'), may hold values from -0.85 to 0.85
- ema_delta: float32 [768, 16], P('ch'), may hold values from -14 to -1.9
- ema_beta: float32 [768, 16], P('ch'), may hold values from -3 to 3
- ema_eta: float32 [768, 16], P('ch'), may hold values from -1.5 to 1.5
- ema_omega: float32 [768], P('ch'), may hold values from -2 to 2
- w_mix: bfloat16 [768, 3200], replicated, may hold values from -0.21875 to 0.21875
- b_mix: float32 [3200], replicated, may hold values from -1.5 to 1.5
- w_value: bfloat16 [768, 1536], replicated, may hold values from -0.21875 to 0.21875
- b_value: float32 [1536], replicated, may hold values from -1.5 to 1.5
- w_out: bfloat16 [1536, 768], replicated, may hold values from -0.3125 to 0.3125
- b_out: float32 [768], replicated, may hold values from -1.5 to 1.5
- qk_scale: float32 [2, 128], replicated, may hold values from 0.25 to 1.75
- qk_shift: float32 [2, 128], replicated, may hold values from -1.5 to 1.5
- ln_gain: float32 [768], replicated, may hold values from 0.5 to 1.5
- ln_bias: float32 [768], replicated, may hold values from -1.5 to 1.5
- w_up: bfloat16 [768, 1536], replicated, may hold values from -0.21875 to 0.21875
- b_up: float32 [1536], replicated, may hold values from -1.5 to 1.5
- w_down: bfloat16 [1536, 768], replicated, may hold values from -0.21875 to 0.21875
- b_down: float32 [768], replicated, may hold values from -1.5 to 1.5
Outputs:
- output: bfloat16 [4, 768, 4096], P(None, 'ch', 'tok')
- input_grad: float32 [4, 768, 4096], P(None, 'ch', 'tok')
- grad_ema_alpha: float32 [768, 16], P('ch')
- grad_ema_delta: float32 [768, 16], P('ch')
- grad_ema_beta: float32 [768, 16], P('ch')
- grad_ema_eta: float32 [768, 16], P('ch')
- grad_ema_omega: float32 [768], P('ch')
- grad_w_mix: float32 [768, 3200], P('ch')
- grad_b_mix: float32 [3200], replicated
- grad_w_value: float32 [768, 1536], P('ch')
- grad_b_value: float32 [1536], replicated
- grad_w_out: float32 [1536, 768], P('ch')
- grad_b_out: float32 [768], replicated
- grad_qk_scale: float32 [2, 128], replicated
- grad_qk_shift: float32 [2, 128], replicated
- grad_ln_gain: float32 [768], replicated
- grad_ln_bias: float32 [768], replicated
- grad_w_up: float32 [768, 1536], P('ch')
- grad_b_up: float32 [1536], replicated
- grad_w_down: float32 [1536, 768], P('ch')
- grad_b_down: float32 [768], replicated
Inputs may be any that keep to these rules, and one draw needn't show every extreme that they name: `seq_lengths`: every sequence but one, chosen by the seed, has 4096 live positions; that one has 2560 or more.
All inputs are finite; a program needn't handle non-finite values.
Results may differ from a plain program's by a relative error of at most 0.025.
The roundings to bfloat16 on the way count: a program that leaves them out, or rounds other values in their place, can miss the bound.
Values may be sent and summed in bfloat16 or wider, within the bound.
No kernel may reach another device: no remote copies, remote signals or barrier semaphores. Data moves between devices by JAX's collectives and lax.ppermute only.
A program may use at most 192 MiB of HBM per device.

v0:
```python
import jax
import jax.numpy as jnp
from jax import lax
from jax.sharding import PartitionSpec as P

GROUP = 128
highest = lax.Precision.HIGHEST


def prefix(shard, axis, combine, identity, reverse):
    size, position = (lax.axis_size(axis), lax.axis_index(axis))
    everything = jax.tree.map(lambda part: lax.all_gather(part, axis), shard)
    start = jax.tree.map(
        lambda part, zero: jnp.broadcast_to(jnp.asarray(zero, part.dtype), part.shape),
        shard,
        identity,
    )

    def lap(k, before):
        at = size - 1 - k if reverse else k
        reached = at > position if reverse else at < position
        new = combine(before, jax.tree.map(lambda part: part[at], everything))
        return jax.tree.map(lambda a, b: jnp.where(reached, a, b), new, before)

    return lax.fori_loop(0, size, lap, start)


def silu_slope(preact):
    sigma = jax.nn.sigmoid(preact)
    return sigma * (1.0 + preact * (1.0 - sigma))


def decay_logs(alpha_logit, delta_logit):
    return jnp.log1p(-jax.nn.sigmoid(alpha_logit) * jax.nn.sigmoid(delta_logit))


def ema_core(seq_f, alpha_logit, delta_logit, beta, eta, omega, state_in):
    nseq_count, channels, local_len = seq_f.shape
    blocks_n = local_len // GROUP
    log_decay = decay_logs(alpha_logit, delta_logit)
    scaled = jax.nn.sigmoid(alpha_logit) * beta
    offsets = jnp.arange(GROUP, dtype=jnp.float32)
    powers = jnp.exp(offsets[None, None, :] * log_decay[:, :, None])
    kernel = jnp.einsum("dj,djt->dt", eta * scaled, powers, precision=highest)
    lag = offsets[:, None] - offsets[None, :]
    onehot = (lag[None] == offsets[:, None, None]).astype(jnp.float32)
    toeplitz = jnp.einsum("dm,mts->dts", kernel, onehot, precision=highest)
    blocks = seq_f.reshape(nseq_count, channels, blocks_n, GROUP)
    inner = jnp.einsum("dts,ndbs->ndbt", toeplitz, blocks, precision=highest)
    state_pow = scaled[:, :, None] * jnp.flip(powers, axis=2)
    running = jnp.einsum("djs,ndbs->ndbj", state_pow, blocks, precision=highest)
    span = 1
    while span < blocks_n:
        factor = jnp.exp(span * GROUP * log_decay)
        moved = jnp.pad(running, ((0, 0), (0, 0), (span, 0), (0, 0)))[:, :, :blocks_n]
        running = running + factor[None, :, None, :] * moved
        span = span * 2
    starts = jnp.pad(running, ((0, 0), (0, 0), (1, 0), (0, 0)))[:, :, :blocks_n]
    group_ids = jnp.arange(blocks_n, dtype=jnp.float32)
    entry = jnp.exp(group_ids[None, :, None] * (GROUP * log_decay)[:, None, :])
    starts = starts + entry[None] * state_in[:, :, None, :]
    carry_pow = eta[:, :, None] * powers * jnp.exp(log_decay)[:, :, None]
    smooth = inner + jnp.einsum("djt,ndbj->ndbt", carry_pow, starts, precision=highest)
    smooth = smooth.reshape(nseq_count, channels, local_len)
    return jax.nn.silu(smooth + omega[None, :, None] * seq_f)


def state_advance(seq_f, alpha_logit, delta_logit, beta, state_in):
    local_len = seq_f.shape[2]
    log_decay = decay_logs(alpha_logit, delta_logit)
    scaled = jax.nn.sigmoid(alpha_logit) * beta
    reverse_pos = jnp.arange(local_len - 1, -1, -1, dtype=jnp.float32)
    weights = scaled[:, :, None] * jnp.exp(reverse_pos[None, None, :] * log_decay[:, :, None])
    fresh = jnp.einsum("djs,nds->ndj", weights, seq_f, precision=highest)
    return jnp.exp(local_len * log_decay)[None] * state_in + fresh


def chain_combine(earlier, later):
    return (earlier[0] * later[0], later[0][None] * earlier[1] + later[1])


def to_rows(columns):
    return jnp.swapaxes(columns, 1, 2).reshape(-1, columns.shape[1])


def from_rows(table, nseq_count):
    return jnp.swapaxes(table.reshape(nseq_count, -1, table.shape[1]), 1, 2)


ORDER_A = (("tok", 1), ("ch", 0))
ORDER_B = (("ch", 0), ("tok", 1))


def bits_of(axis):
    return lax.axis_size(axis).bit_length() - 1


def exchange(part, axis, bit):
    size = lax.axis_size(axis)
    return lax.ppermute(part, axis, [(i, i ^ 1 << bit) for i in range(size)])


def reduce_rows(grad, order):
    parts, rows, columns = grad.shape
    ch_bits, tok_bits = (bits_of("ch"), bits_of("tok"))
    own = rows >> ch_bits + tok_bits
    names = [("ch", k) for k in reversed(range(ch_bits))] + [
        ("tok", k) for k in reversed(range(tok_bits))
    ]
    stages = [("tok", 0)] + list(order)
    stages += [name for name in reversed(names) if name not in stages]
    kept = grad.reshape((parts,) + (2,) * len(names) + (own, columns))
    arrived = None
    for axis, bit in stages:
        at = 1 + names.index((axis, bit))
        mine = lax.axis_index(axis) >> bit & 1

        def pick(which):
            half = lax.dynamic_index_in_dim(kept, which, at, keepdims=False)
            if arrived is None:
                return half
            other = lax.dynamic_index_in_dim(arrived, which, at, keepdims=False)
            return (half.astype(jnp.float32) + other.astype(jnp.float32)).astype(jnp.bfloat16)

        sent, kept = (pick(1 - mine), pick(mine))
        names.remove((axis, bit))
        arrived = exchange(sent, axis, bit)
    total = (kept.astype(jnp.float32) + arrived.astype(jnp.float32)).astype(jnp.bfloat16)
    whole = lax.all_gather(total, "tok", axis=1)
    return whole.reshape(parts, -1, columns).astype(jnp.float32)


def reduce_pair(wide, tall, order):
    rows, columns = tall.shape
    low = jnp.bfloat16
    merged = jnp.stack([wide.astype(low).reshape(rows, columns), tall.astype(low)])
    merged = reduce_rows(merged, order)
    return (merged[0].reshape(-1, wide.shape[1]), merged[1])


def local(
    inputs,
    out_grad,
    seq_lengths,
    ema_alpha,
    ema_delta,
    ema_beta,
    ema_eta,
    ema_omega,
    w_mix,
    b_mix,
    w_value,
    b_value,
    w_out,
    b_out,
    qk_scale,
    qk_shift,
    ln_gain,
    ln_bias,
    w_up,
    b_up,
    w_down,
    b_down,
):
    nseq_count, channels, local_len = inputs.shape
    width = w_mix.shape[0]
    zwidth = qk_scale.shape[1]
    vwidth = w_value.shape[1]
    scale = zwidth ** (-0.5)
    tok_index = lax.axis_index("tok")
    seq_f = inputs.astype(jnp.float32)
    log_total = local_len * decay_logs(ema_alpha, ema_delta)
    decay_all = jnp.exp(log_total)
    zero_state = jnp.zeros((nseq_count, channels, ema_alpha.shape[1]), jnp.float32)
    state_dev = state_advance(seq_f, ema_alpha, ema_delta, ema_beta, zero_state)
    state_in = prefix(
        (decay_all, state_dev), "tok", chain_combine, (jnp.ones_like(decay_all), zero_state), False
    )[1]
    activ = ema_core(seq_f, ema_alpha, ema_delta, ema_beta, ema_eta, ema_omega, state_in)
    recv_in, recv_mix = (
        lax.all_to_all(inputs, "ch", split_axis=2, concat_axis=1, tiled=True),
        lax.all_to_all(activ.astype(jnp.bfloat16), "ch", split_axis=2, concat_axis=1, tiled=True),
    )
    tok_in = to_rows(recv_in)
    tok_mix = to_rows(recv_mix)
    row_count = tok_in.shape[0]
    blocks_n = row_count // GROUP
    value_pre = jnp.dot(tok_in, w_value, preferred_element_type=jnp.float32) + b_value
    values = jax.nn.silu(value_pre).astype(jnp.bfloat16)
    mix_pre = jnp.dot(tok_mix, w_mix, preferred_element_type=jnp.float32) + b_mix
    gate_pre = mix_pre[:, :width]
    query_pre = mix_pre[:, width : width + zwidth]
    reset_pre = mix_pre[:, width + zwidth : width + zwidth + vwidth]
    hidden_mix = mix_pre[:, width + zwidth + vwidth :]
    update = jax.nn.sigmoid(gate_pre)
    shared = jax.nn.silu(query_pre)
    queries = (shared * qk_scale[0] + qk_shift[0]).astype(jnp.bfloat16)
    keys_all = (shared * qk_scale[1] + qk_shift[1]).astype(jnp.bfloat16)
    reset = jax.nn.silu(reset_pre)
    query_blk = queries.reshape(blocks_n, GROUP, zwidth)
    key_blk = keys_all.reshape(blocks_n, GROUP, zwidth)
    value_blk = values.reshape(blocks_n, GROUP, vwidth)
    position = jnp.arange(GROUP)
    causal = position[:, None] >= position[None, :]

    def block_scores():
        raw = (
            jnp.einsum("cqz,ckz->cqk", query_blk, key_blk, preferred_element_type=jnp.float32)
            * scale
        )
        return jnp.where(causal[None], raw, -1e30)

    scores = block_scores()
    top_score = jnp.max(scores, axis=-1, keepdims=True)
    log_norm = top_score + jnp.log(jnp.sum(jnp.exp(scores - top_score), axis=-1, keepdims=True))
    probs_bf = jnp.exp(scores - log_norm).astype(jnp.bfloat16)
    attended = jnp.einsum(
        "cqk,ckv->cqv", probs_bf, value_blk, preferred_element_type=jnp.float32
    ).reshape(row_count, vwidth)
    gated = (reset * attended).astype(jnp.bfloat16)
    hidden_pre = hidden_mix + jnp.dot(gated, w_out, preferred_element_type=jnp.float32) + b_out
    hidden = jax.nn.silu(hidden_pre)
    resid = tok_in.astype(jnp.float32)
    blend = update * hidden + (1.0 - update) * resid
    centered = blend - jnp.mean(blend, axis=-1, keepdims=True)
    rstd = lax.rsqrt(jnp.mean(centered * centered, axis=-1, keepdims=True) + 1e-05)
    unit = centered * rstd
    normed = unit * ln_gain + ln_bias
    normed_bf = normed.astype(jnp.bfloat16)
    ffn_pre = jnp.dot(normed_bf, w_up, preferred_element_type=jnp.float32) + b_up
    ffn_hidden = jax.nn.silu(ffn_pre).astype(jnp.bfloat16)
    result = normed + jnp.dot(ffn_hidden, w_down, preferred_element_type=jnp.float32) + b_down
    out_local = lax.all_to_all(
        from_rows(result.astype(jnp.bfloat16), nseq_count),
        "ch",
        split_axis=1,
        concat_axis=2,
        tiled=True,
    )
    seq_pos = tok_index * local_len + jnp.arange(local_len, dtype=jnp.int32)
    live = (seq_pos[None, :] < seq_lengths[:, None])[:, None, :]
    output = jnp.where(live, out_local, jnp.zeros_like(out_local))
    grad_masked = jnp.where(live, out_grad, jnp.zeros_like(out_grad))
    grad_rows = to_rows(lax.all_to_all(grad_masked, "ch", split_axis=2, concat_axis=1, tiled=True))
    grad_f = grad_rows.astype(jnp.float32)
    g_down = jnp.dot(ffn_hidden.T, grad_rows, preferred_element_type=jnp.float32)
    g_bdown = jnp.sum(grad_f, axis=0)
    d_ffn = (
        jnp.dot(grad_rows, w_down.T, preferred_element_type=jnp.float32) * silu_slope(ffn_pre)
    ).astype(jnp.bfloat16)
    g_up = jnp.dot(normed_bf.T, d_ffn, preferred_element_type=jnp.float32)
    g_bup = jnp.sum(d_ffn.astype(jnp.float32), axis=0)
    d_normed = grad_f + jnp.dot(d_ffn, w_up.T, preferred_element_type=jnp.float32)
    g_gain = jnp.sum(d_normed * unit, axis=0)
    g_lnbias = jnp.sum(d_normed, axis=0)
    d_unit = d_normed * ln_gain
    d_blend = rstd * (
        d_unit
        - jnp.mean(d_unit, axis=-1, keepdims=True)
        - unit * jnp.mean(d_unit * unit, axis=-1, keepdims=True)
    )
    d_hidden_pre = (d_blend * update * silu_slope(hidden_pre)).astype(jnp.bfloat16)
    d_update_pre = d_blend * (hidden - resid) * update * (1.0 - update)
    d_direct = d_blend * (1.0 - update)
    g_out = jnp.dot(gated.T, d_hidden_pre, preferred_element_type=jnp.float32)
    g_bout = jnp.sum(d_hidden_pre.astype(jnp.float32), axis=0)
    d_gated = jnp.dot(d_hidden_pre, w_out.T, preferred_element_type=jnp.float32)
    d_reset_pre = d_gated * attended * silu_slope(reset_pre)
    d_attended = (d_gated * reset).astype(jnp.bfloat16).reshape(blocks_n, GROUP, vwidth)
    scores = block_scores()
    probs = jnp.exp(scores - log_norm)
    probs_bf = probs.astype(jnp.bfloat16)
    d_probs = jnp.einsum("cqv,ckv->cqk", d_attended, value_blk, preferred_element_type=jnp.float32)
    d_values = jnp.einsum(
        "cqk,cqv->ckv", probs_bf, d_attended, preferred_element_type=jnp.float32
    ).reshape(row_count, vwidth)
    d_scores = (probs * (d_probs - jnp.sum(d_probs * probs, axis=-1, keepdims=True))).astype(
        jnp.bfloat16
    )
    d_query = (
        jnp.einsum("cqk,ckz->cqz", d_scores, key_blk, preferred_element_type=jnp.float32).reshape(
            row_count, zwidth
        )
        * scale
    )
    d_key = (
        jnp.einsum("cqk,cqz->ckz", d_scores, query_blk, preferred_element_type=jnp.float32).reshape(
            row_count, zwidth
        )
        * scale
    )
    d_value_pre = (d_values * silu_slope(value_pre)).astype(jnp.bfloat16)
    g_value = jnp.dot(tok_in.T, d_value_pre, preferred_element_type=jnp.float32)
    g_bvalue = jnp.sum(d_value_pre.astype(jnp.float32), axis=0)
    d_resid = d_direct + jnp.dot(d_value_pre, w_value.T, preferred_element_type=jnp.float32)
    g_qscale = jnp.stack([jnp.sum(d_query * shared, axis=0), jnp.sum(d_key * shared, axis=0)])
    g_qshift = jnp.stack([jnp.sum(d_query, axis=0), jnp.sum(d_key, axis=0)])
    d_query_pre = (d_query * qk_scale[0] + d_key * qk_scale[1]) * silu_slope(query_pre)
    d_mix_pre = jnp.concatenate(
        [d_update_pre, d_query_pre, d_reset_pre, d_hidden_pre.astype(jnp.float32)], axis=1
    ).astype(jnp.bfloat16)
    g_mix = jnp.dot(tok_mix.T, d_mix_pre, preferred_element_type=jnp.float32)
    g_bmix = jnp.sum(d_mix_pre.astype(jnp.float32), axis=0)
    d_mix_in = jnp.dot(d_mix_pre, w_mix.T, preferred_element_type=jnp.float32)
    back_resid, back_mix = (
        lax.all_to_all(
            from_rows(d_resid.astype(jnp.bfloat16), nseq_count),
            "ch",
            split_axis=1,
            concat_axis=2,
            tiled=True,
        ),
        lax.all_to_all(
            from_rows(d_mix_in.astype(jnp.bfloat16), nseq_count),
            "ch",
            split_axis=1,
            concat_axis=2,
            tiled=True,
        ),
    )
    _, ema_pull = jax.vjp(
        ema_core, seq_f, ema_alpha, ema_delta, ema_beta, ema_eta, ema_omega, state_in
    )
    dx_ema, ga_first, gd_first, gb_first, g_eta, g_omega, state_grad = ema_pull(
        back_mix.astype(jnp.float32)
    )
    later_grad = prefix(
        (decay_all, state_grad), "tok", chain_combine, (jnp.ones_like(decay_all), zero_state), True
    )[1]
    _, state_pull = jax.vjp(state_advance, seq_f, ema_alpha, ema_delta, ema_beta, state_in)
    dx_state, ga_second, gd_second, gb_second, unused_grad = state_pull(later_grad)
    input_grad = back_resid.astype(jnp.float32) + dx_ema + dx_state
    g_up_s, g_down_s = reduce_pair(g_up, g_down, ORDER_A)
    g_value_s, g_out_s = reduce_pair(g_value, g_out, ORDER_B)
    g_mix_s = reduce_rows(g_mix.astype(jnp.bfloat16)[None], ORDER_A)[0]
    ema_grads = lax.psum(
        (ga_first + ga_second, gd_first + gd_second, gb_first + gb_second, g_eta, g_omega), "tok"
    )
    summed = (g_mix_s, g_value_s, g_out_s, g_up_s, g_down_s) + ema_grads
    smalls = lax.psum(
        (g_bmix, g_bvalue, g_bout, g_qscale, g_qshift, g_gain, g_lnbias, g_bup, g_bdown),
        ("ch", "tok"),
    )
    return (
        output,
        input_grad,
        summed[5],
        summed[6],
        summed[7],
        summed[8],
        summed[9],
        summed[0],
        smalls[0],
        summed[1],
        smalls[1],
        summed[2],
        smalls[2],
        smalls[3],
        smalls[4],
        smalls[5],
        smalls[6],
        summed[3],
        smalls[7],
        summed[4],
        smalls[8],
    )


def solution(mesh):
    placed = (
        P(None, "ch", "tok"),
        P(None, "ch", "tok"),
        P(),
        P("ch", None),
        P("ch", None),
        P("ch", None),
        P("ch", None),
        P("ch"),
        P(),
        P(),
        P(),
        P(),
        P(),
        P(),
        P(),
        P(),
        P(),
        P(),
        P(),
        P(),
        P(),
        P(),
    )
    return jax.shard_map(
        local,
        mesh=mesh,
        in_specs=placed,
        out_specs=(
            P(None, "ch", "tok"),
            P(None, "ch", "tok"),
            P("ch", None),
            P("ch", None),
            P("ch", None),
            P("ch", None),
            P("ch"),
            P("ch", None),
            P(),
            P("ch", None),
            P(),
            P("ch", None),
            P(),
            P(),
            P(),
            P(),
            P(),
            P("ch", None),
            P(),
            P("ch", None),
            P(),
        ),
        check_vma=False,
    )
```

profile of v0, /device:TPU:0, one launch (start us, length us, event | category | flops | bytes accessed | tf_op | source)
XLA Modules:
  0.0 585.6 jit_solution(6185668429854411058)
XLA Ops:
  3.2 7.3 %all-to-all-start.1 = ((bf16[4,96,1024]{1,0,2:T(4,128)(2,1)}), bf16[4,96,1024]{1,0,2:T(4,128)(2,1)}, u32[]{:S(2)}, u32[]{:S(2)}) async-start(bf16[4,96,1024]{1,0,2:T(4,128)(2,1)} %copy.451), calls=%async_computation.1 | async-start | bytes 2097152 | tf_op jit(solution)/shard_map/all_to_all | solution.py:181
  15.4 5.6 all-gather.6
  29.1 6.0 %all-gather.1 = f32[16,96,16]{1,2,0:T(8,128)S(1)} all-gather(f32[4,96,16]{1,2,0:T(8,128)S(1)} %copy.442), channel_id=3, replica_groups=mesh['ch'=8,'tok'=4] {'tok'}, dimensions={0}, use_global_device_ids=true | all-gather | bytes 122880 | tf_op jit(solution)/shard_map/all_gather | solution.py:12
  35.1 7.5 %while.30 = (s32[]{:T(128)}, f32[4,96,16]{1,2,0:T(8,128)}, s32[]{:T(128)}, f32[4,96,16]{1,2,0:T(8,128)}, f32[4,4,96,16]{2,3,1,0:T(8,128)S(1)}, /*index=5*/s32[]{:T(128)}, s32[]{:T(128)}) while((s32[]{:T(128)}, f32[4,96,16]{1,2,0:T(8,128)}, s32[]{:T(128)}, f32[4,96,16]{1,2,0:T(8,128)}, f32[4,4,96,16]{2,3,1,0:T(8,128)S(1)}, ...), condition=%wide.region_1.2_spmd.clone, body=%wide.region_0.1_spmd.clone.sunk | while | flops 24580 | bytes 92273 | solution.py:25
  65.4 10.1 %bitcast_add_fusion.3 = f32[4,96,8,128]{3,2,0,1:T(8,128)} fusion(f32[96,4,8,128]{3,2,1,0:T(8,128)S(1)} %fusion.92, f32[96,128,128,1]{2,0,1,3:T(8,128)} %fusion.29, bf16[4,96,8,128]{3,2,1,0:T(8,128)(2,1)S(1)} %bitcast.447), kind=kOutput, calls=%fused_computation.130 | convolution fusion | flops 604372992 | bytes 10223616 | tf_op jit(solution)/shard_map/dts,ndbs->ndbt/dot_general | solution.py:49
  85.3 6.2 %all-to-all-start = ((bf16[4,96,1024]{1,0,2:T(4,128)(2,1)}), bf16[4,96,1024]{1,0,2:T(4,128)(2,1)}, u32[]{:S(2)}, u32[]{:S(2)}) async-start(bf16[4,96,1024]{1,0,2:T(4,128)(2,1)} %copy.447), calls=%async_computation | async-start | bytes 2097152 | tf_op jit(solution)/shard_map/all_to_all | solution.py:182
  96.2 21.6 %all-to-all-done = bf16[4,96,1024]{1,0,2:T(4,128)(2,1)} async-done(((bf16[4,96,1024]{1,0,2:T(4,128)(2,1)}), bf16[4,96,1024]{1,0,2:T(4,128)(2,1)}, u32[]{:S(2)}, u32[]{:S(2)}) %all-to-all-start) | async-done | bytes 786464 | tf_op jit(solution)/shard_map/all_to_all | solution.py:182
  122.5 5.6 convolution_add_fusion
  151.0 19.9 %all-to-all-done.2 = bf16[4,768,128]{2,0,1:T(4,128)(2,1)} async-done(((bf16[4,768,128]{2,0,1:T(4,128)(2,1)}), bf16[4,768,128]{2,0,1:T(4,128)(2,1)}, u32[]{:S(2)}, u32[]{:S(2)}) %all-to-all-start.2) | async-done | bytes 786464 | tf_op jit(solution)/shard_map/all_to_all | solution.py:233
  180.8 24.8 %all-to-all-done.3 = bf16[4,96,1024]{1,0,2:T(4,128)(2,1)} async-done(((bf16[4,96,1024]{1,0,2:T(4,128)(2,1)}), bf16[4,96,1024]{1,0,2:T(4,128)(2,1)}, u32[]{:S(2)}, u32[]{:S(2)}) %all-to-all-start.3) | async-done | bytes 786464 | tf_op jit(solution)/shard_map/all_to_all | solution.py:244
  238.4 6.7 %convolution_convert_fusion.5 = bf16[512,768]{1,0:T(8,128)(2,1)} fusion(bf16[768,3200]{1,0:T(8,128)(2,1)} %param.34, bf16[512,768]{1,0:T(8,128)(2,1)S(1)} %copy-done.43, bf16[512,1536]{1,0:T(8,128)(2,1)} %get-tuple-element.511, bf16[512,128]{1,0:T(8,128)(2,1)S(1)} %get-tuple-element.513, bf16[512,768]{1,0:T(8,128)(2,1)S(1)} %copy-done.45), kind=kOutput, calls=%fused_computation.158 | convolution fusion | flops 2530082816 | bytes 8978432 | tf_op jit(solution)/shard_map/dot_general | solution.py:304
  290.9 42.2 %all-reduce.8 = (f32[3200]{0:T(1024)}, f32[1536]{0:T(1024)}, f32[768]{0:T(1024)}, f32[2,128]{1,0:T(2,128)}, f32[2,128]{1,0:T(2,128)}, /*index=5*/f32[768]{0:T(10...) all-reduce(f32[3200]{0:T(1024)S(1)} %convert_reduce_fusion, ...), channel_id=1, replica_groups=mesh['ch'=8,'tok'=4] {'ch','tok'}, use_global_device_ids=true, to_apply=%region_31.32 | all-reduce | flops 9856 | bytes 78848 | tf_op jit(solution)/shard_map/psum | solution.py:340
  382.8 5.6 multiply_reduce_fusion
  400.7 11.5 %add_bitcast_fusion = f32[4,96,8,128]{3,2,0,1:T(8,128)} fusion(f32[96,4,8,128]{3,2,1,0:T(8,128)} %fusion.95, f32[96,128,128,1]{2,0,1,3:T(8,128)} %fusion.29, f32[4,96,8,128]{3,2,0,1:T(8,128)} %reshape.712), kind=kOutput, calls=%fused_computation.139 | convolution fusion | flops 604372992 | bytes 11010048 | tf_op jit(solution)/shard_map/transpose(jvp(dts,ndbs->ndbt))/dot_general | solution.py:49
  422.6 6.5 %convolution_bitcast_fusion = f32[96,128,128]{2,1,0:T(8,128)S(1)} fusion(f32[4,96,8,128]{3,2,0,1:T(8,128)} %reshape.712, bf16[4,96,8,128]{3,2,1,0:T(8,128)(2,1)S(1)} %bitcast.449), kind=kOutput, calls=%fused_computation.78 | convolution fusion | flops 603979776 | bytes 8650752 | tf_op jit(solution)/shard_map/transpose(jvp(dts,ndbs->ndbt))/dot_general | solution.py:49
  429.1 7.9 %fusion.2 = f32[96,128,1]{1,0,2:T(8,128)S(1)} fusion(f32[96,128,128]{2,1,0:T(8,128)S(1)} %convolution_bitcast_fusion, f32[128,128]{1,0:T(8,128)S(1)} %copy-done.84), kind=kOutput, calls=%fused_computation.7 | convolution fusion | flops 2418016256 | bytes 6406144 | tf_op jit(solution)/shard_map/transpose(jvp(dm,mts->dts))/dot_general | solution.py:47
  462.9 6.8 %bitcast_add_fusion.2 = f32[4,96,1024]{2,0,1:T(4,128)S(1)} fusion(f32[4,96,1024]{2,0,1:T(4,128)} %reshape.714, f32[4,96,1024]{2,0,1:T(4,128)} %reshape.713, f32[4,96,1024]{2,0,1:T(4,128)} %get-tuple-element.501, f32[96,4,16]{2,1,0:T(4,128)S(1)} %copy-done.101, f32[96,16]{1,0:T(8,128)S(1)} %copy-done.78, f32[1024]{0:T(1024)S(1)} %copy-done.129, ...), kind=kOutput, calls=%fused_computation.123 | convolution fusion | flops 80216064 | bytes 6332800 | tf_op jit(solution)/shard_map/transpose(jvp(djs,nds->ndj))/dot_general | solution.py:74
  482.9 17.9 %collective-permute-done.1 = bf16[1,2,2,2,24,3200]{5,4,1,3,2,0:T(8,128)(2,1)} collective-permute-done((bf16[1,2,2,2,24,3200]{5,4,1,3,2,0:T(8,128)(2,1)}, bf16[1,2,2,2,24,3200]{5,4,1,3,2,0:T(8,128)(2,1)}, u32[]{:S(2)}, u32[]{:S(2)}) %collective-permute-start.1) | collective-permute-done | bytes 1228832 | tf_op jit(solution)/shard_map/ppermute | solution.py:100
  507.7 13.2 %all-reduce.9 = (f32[96,16]{0,1:T(8,128)}, f32[96,16]{0,1:T(8,128)}, f32[96,16]{0,1:T(8,128)}, f32[96,16]{0,1:T(8,128)}, f32[96]{0:T(128)}) all-reduce(f32[96,16]{0,1:T(8,128)S(1)} %get-tuple-element.537, f32[96,16]{0,1:T(8,128)S(1)} %get-tuple-element.536, ...), channel_id=1, replica_groups=mesh['ch'=8,'tok'=4] {'tok'}, use_global_device_ids=true, to_apply=%region_23.24 | all-reduce | flops 6240 | bytes 49920 | tf_op jit(solution)/shard_map/psum | solution.py:336
  527.5 6.1 %collective-permute-done.13 = bf16[2,2,48,768]{3,2,0,1:T(8,128)(2,1)S(1)} collective-permute-done((bf16[2,2,48,768]{3,2,0,1:T(8,128)(2,1)S(1)}, bf16[2,2,48,768]{3,2,0,1:T(8,128)(2,1)S(1)}, u32[]{:S(2)}, u32[]{:S(2)}) %collective-permute-start.13) | collective-permute-done | bytes 294944 | tf_op jit(solution)/shard_map/ppermute | solution.py:100
  543.5 8.5 %all-gather.5 = bf16[2,192,768]{2,1,0:T(8,128)(2,1)S(1)} all-gather(bf16[2,48,768]{2,1,0:T(8,128)(2,1)S(1)} %fusion.144), channel_id=7, replica_groups=mesh['ch'=8,'tok'=4] {'tok'}, dimensions={1}, use_global_device_ids=true | all-gather | bytes 737280 | tf_op jit(solution)/shard_map/all_gather | solution.py:129
  552.0 7.7 %all-gather.4 = bf16[2,192,768]{2,1,0:T(8,128)(2,1)S(1)} all-gather(bf16[2,48,768]{2,1,0:T(8,128)(2,1)S(1)} %fusion.147), channel_id=6, replica_groups=mesh['ch'=8,'tok'=4] {'tok'}, dimensions={1}, use_global_device_ids=true | all-gather | bytes 737280 | tf_op jit(solution)/shard_map/all_gather | solution.py:129
  567.8 8.5 %collective-permute-done.4 = bf16[1,24,3200]{2,1,0:T(8,128)(2,1)S(1)} collective-permute-done((bf16[1,24,3200]{2,1,0:T(8,128)(2,1)S(1)}, bf16[1,24,3200]{2,1,0:T(8,128)(2,1)S(1)}, u32[]{:S(2)}, u32[]{:S(2)}) %collective-permute-start.4) | collective-permute-done | bytes 153632 | tf_op jit(solution)/shard_map/ppermute | solution.py:100
  577.2 7.0 %all-gather.3 = bf16[4,24,3200]{2,1,0:T(8,128)(2,1)S(1)} all-gather(bf16[1,24,3200]{2,1,0:T(8,128)(2,1)S(1)} %fusion.139), channel_id=5, replica_groups=mesh['ch'=8,'tok'=4] {'tok'}, dimensions={0}, use_global_device_ids=true | all-gather | bytes 768000 | tf_op jit(solution)/shard_map/all_gather | solution.py:129
  (522 shorter events, 322.6 us)
Async XLA Ops:
  0.7 135.2 %copy-start = (bf16[1536,768]{1,0:T(8,128)(2,1)S(1)}, bf16[1536,768]{1,0:T(8,128)(2,1)}, u32[]{:S(2)}) copy-start(bf16[1536,768]{1,0:T(8,128)(2,1)} %param.38) | copy-start | bytes 7077892
  3.2 82.1 %all-to-all-start.1 = ((bf16[4,96,1024]{1,0,2:T(4,128)(2,1)}), bf16[4,96,1024]{1,0,2:T(4,128)(2,1)}, u32[]{:S(2)}, u32[]{:S(2)}) async-start(bf16[4,96,1024]{1,0,2:T(4,128)(2,1)} %copy.451), calls=%async_computation.1 | async-start | bytes 2097152 | tf_op jit(solution)/shard_map/all_to_all | solution.py:181
  85.3 32.5 %all-to-all-start = ((bf16[4,96,1024]{1,0,2:T(4,128)(2,1)}), bf16[4,96,1024]{1,0,2:T(4,128)(2,1)}, u32[]{:S(2)}, u32[]{:S(2)}) async-start(bf16[4,96,1024]{1,0,2:T(4,128)(2,1)} %copy.447), calls=%async_computation | async-start | bytes 2097152 | tf_op jit(solution)/shard_map/all_to_all | solution.py:182
  146.4 24.4 %all-to-all-start.2 = ((bf16[4,768,128]{2,0,1:T(4,128)(2,1)}), bf16[4,768,128]{2,0,1:T(4,128)(2,1)}, u32[]{:S(2)}, u32[]{:S(2)}) async-start(bf16[4,768,128]{2,0,1:T(4,128)(2,1)} %bitcast.466), calls=%async_computation.2 | async-start | bytes 1572864 | tf_op jit(solution)/shard_map/all_to_all | solution.py:233
  175.8 29.8 %all-to-all-start.3 = ((bf16[4,96,1024]{1,0,2:T(4,128)(2,1)}), bf16[4,96,1024]{1,0,2:T(4,128)(2,1)}, u32[]{:S(2)}, u32[]{:S(2)}) async-start(bf16[4,96,1024]{1,0,2:T(4,128)(2,1)} %copy.459), calls=%async_computation.3 | async-start | bytes 2097152 | tf_op jit(solution)/shard_map/all_to_all | solution.py:244
  264.4 75.2 %all-to-all-start.5 = ((bf16[4,768,128]{2,0,1:T(4,128)(2,1)}), bf16[4,768,128]{2,0,1:T(4,128)(2,1)}, u32[]{:S(2)}, u32[]{:S(2)}) async-start(bf16[4,768,128]{2,0,1:T(4,128)(2,1)} %bitcast.54), calls=%async_computation.5 | async-start | bytes 1572864 | tf_op jit(solution)/shard_map/all_to_all | solution.py:313
  284.4 156.8 %collective-permute-start.10 = (bf16[2,2,2,2,2,48,768]{6,5,0,1,3,2,4:T(8,128)(2,1)}, bf16[2,2,2,2,2,48,768]{6,5,0,1,3,2,4:T(8,128)(2,1)}, u32[]{:S(2)}, u32[]{:S(2)}) collective-permute-start(bf16[2,2,2,2,2,48,768]{6,5,0,1,3,2,4:T(8,128)(2,1)} %copy_bitcast_fusion.1), channel_id=1, source_target_pairs={{0,1},{1,0},{2,3},{3,2},{4,5},{5,4},{6,7},{7,6},{8,9},{9,8},{10,11... | collective-permute-start | bytes 7077896 | tf_op jit(solution)/shard_map/ppermute | solution.py:100
  286.0 160.6 %collective-permute-start.5 = (bf16[2,2,2,2,2,48,768]{6,5,0,1,4,2,3:T(8,128)(2,1)}, bf16[2,2,2,2,2,48,768]{6,5,0,1,4,2,3:T(8,128)(2,1)}, u32[]{:S(2)}, u32[]{:S(2)}) collective-permute-start(bf16[2,2,2,2,2,48,768]{6,5,0,1,4,2,3:T(8,128)(2,1)} %copy_bitcast_fusion.2), channel_id=1, source_target_pairs={{0,1},{1,0},{2,3},{3,2},{4,5},{5,4},{6,7},{7,6},{8,9},{9,8},{10,11... | collective-permute-start | bytes 7077896 | tf_op jit(solution)/shard_map/ppermute | solution.py:100
  290.0 161.1 %collective-permute-start = (bf16[1,2,2,2,2,24,3200]{6,5,1,3,2,4,0:T(8,128)(2,1)}, bf16[1,2,2,2,2,24,3200]{6,5,1,3,2,4,0:T(8,128)(2,1)}, u32[]{:S(2)}, u32[]{:S(2)}) collective-permute-start(bf16[1,2,2,2,2,24,3200]{6,5,1,3,2,4,0:T(8,128)(2,1)} %copy_bitcast_fusion), channel_id=1, source_target_pairs={{0,1},{1,0},{2,3},{3,2},{4,5},{5,4},{6,7},{7,6},{8,9},{9,8},{10,11... | collective-permute-start | bytes 7372808 | tf_op jit(solution)/shard_map/ppermute | solution.py:100
  339.6 51.8 %all-to-all-start.4 = ((bf16[4,768,128]{2,0,1:T(4,128)(2,1)}), bf16[4,768,128]{2,0,1:T(4,128)(2,1)}, u32[]{:S(2)}, u32[]{:S(2)}) async-start(bf16[4,768,128]{2,0,1:T(4,128)(2,1)} %bitcast.465), calls=%async_computation.4 | async-start | bytes 1572864 | tf_op jit(solution)/shard_map/all_to_all | solution.py:306
  445.4 29.1 %collective-permute-start.11 = (bf16[2,2,2,2,48,768]{5,4,0,1,3,2:T(8,128)(2,1)}, bf16[2,2,2,2,48,768]{5,4,0,1,3,2:T(8,128)(2,1)}, u32[]{:S(2)}, u32[]{:S(2)}) collective-permute-start(bf16[2,2,2,2,48,768]{5,4,0,1,3,2:T(8,128)(2,1)} %get-tuple-element.529), channel_id=1, source_target_pairs={{0,2},{1,3},{2,0},{3,1},{4,6},{5,7},{6,4},{7,5},{8,10},{9,11},{10,... | collective-permute-start | bytes 3538952 | tf_op jit(solution)/shard_map/ppermute | solution.py:100
  449.1 30.6 %collective-permute-start.6 = (bf16[2,2,2,2,48,768]{5,4,3,2,1,0:T(8,128)(2,1)}, bf16[2,2,2,2,48,768]{5,4,3,2,1,0:T(8,128)(2,1)}, u32[]{:S(2)}, u32[]{:S(2)}) collective-permute-start(bf16[2,2,2,2,48,768]{5,4,3,2,1,0:T(8,128)(2,1)} %fusion.36), channel_id=1, source_target_pairs={{0,4},{4,0},{8,12},{12,8},{16,20},{20,16},{24,28},{28,24},{1,5},{5... | collective-permute-start | bytes 3538952 | tf_op jit(solution)/shard_map/ppermute | solution.py:100
  455.1 45.7 %collective-permute-start.1 = (bf16[1,2,2,2,24,3200]{5,4,1,3,2,0:T(8,128)(2,1)}, bf16[1,2,2,2,24,3200]{5,4,1,3,2,0:T(8,128)(2,1)}, u32[]{:S(2)}, u32[]{:S(2)}) collective-permute-start(bf16[1,2,2,2,24,3200]{5,4,1,3,2,0:T(8,128)(2,1)} %get-tuple-element.525), channel_id=1, source_target_pairs={{0,2},{1,3},{2,0},{3,1},{4,6},{5,7},{6,4},{7,5},{8,10},{9,11},{10,... | collective-permute-start | bytes 3686408 | tf_op jit(solution)/shard_map/ppermute | solution.py:100
  476.9 24.0 %copy-start.31 = (bf16[1,2,2,2,24,3200]{5,4,1,3,2,0:T(8,128)(2,1)S(1)}, bf16[1,2,2,2,24,3200]{5,4,1,3,2,0:T(8,128)(2,1)}, u32[]{:S(2)}) copy-start(bf16[1,2,2,2,24,3200]{5,4,1,3,2,0:T(8,128)(2,1)} %get-tuple-element.524) | copy-start | bytes 3686404
  477.7 43.2 %collective-permute-start.12 = (bf16[2,2,2,48,768]{4,3,0,2,1:T(8,128)(2,1)}, bf16[2,2,2,48,768]{4,3,0,2,1:T(8,128)(2,1)}, u32[]{:S(2)}, u32[]{:S(2)}) collective-permute-start(bf16[2,2,2,48,768]{4,3,0,2,1:T(8,128)(2,1)} %copy.509), channel_id=1, source_target_pairs={{0,4},{4,0},{8,12},{12,8},{16,20},{20,16},{24,28},{28,24},{1,5},{5... | collective-permute-start | bytes 1769480 | tf_op jit(solution)/shard_map/ppermute | solution.py:100
  481.7 43.6 %collective-permute-start.7 = (bf16[2,2,2,48,768]{4,3,2,1,0:T(8,128)(2,1)}, bf16[2,2,2,48,768]{4,3,2,1,0:T(8,128)(2,1)}, u32[]{:S(2)}, u32[]{:S(2)}) collective-permute-start(bf16[2,2,2,48,768]{4,3,2,1,0:T(8,128)(2,1)} %fusion.116), channel_id=1, source_target_pairs={{0,2},{1,3},{2,0},{3,1},{4,6},{5,7},{6,4},{7,5},{8,10},{9,11},{10,... | collective-permute-start | bytes 1769480 | tf_op jit(solution)/shard_map/ppermute | solution.py:100
  503.5 32.0 %collective-permute-start.2 = (bf16[1,2,2,24,3200]{4,3,2,1,0:T(8,128)(2,1)}, bf16[1,2,2,24,3200]{4,3,2,1,0:T(8,128)(2,1)}, u32[]{:S(2)}, u32[]{:S(2)}) collective-permute-start(bf16[1,2,2,24,3200]{4,3,2,1,0:T(8,128)(2,1)} %copy.493), channel_id=1, source_target_pairs={{0,4},{4,0},{8,12},{12,8},{16,20},{20,16},{24,28},{28,24},{1,5},{5... | collective-permute-start | bytes 1843208 | tf_op jit(solution)/shard_map/ppermute | solution.py:100
  522.1 11.6 %collective-permute-start.13 = (bf16[2,2,48,768]{3,2,0,1:T(8,128)(2,1)S(1)}, bf16[2,2,48,768]{3,2,0,1:T(8,128)(2,1)S(1)}, u32[]{:S(2)}, u32[]{:S(2)}) collective-permute-start(bf16[2,2,48,768]{3,2,0,1:T(8,128)(2,1)S(1)} %get-tuple-element.533), channel_id=1, source_target_pairs={{0,8},{4,12},{8,0},{12,4},{16,24},{20,28},{24,16},{28,20},{1,9},{5... | collective-permute-start | bytes 884744 | tf_op jit(solution)/shard_map/ppermute | solution.py:100
  526.4 16.5 %collective-permute-start.8 = (bf16[2,2,48,768]{3,2,1,0:T(8,128)(2,1)S(1)}, bf16[2,2,48,768]{3,2,1,0:T(8,128)(2,1)S(1)}, u32[]{:S(2)}, u32[]{:S(2)}) collective-permute-start(bf16[2,2,48,768]{3,2,1,0:T(8,128)(2,1)S(1)} %fusion.141), channel_id=1, source_target_pairs={{0,8},{4,12},{8,0},{12,4},{16,24},{20,28},{24,16},{28,20},{1,9},{5... | collective-permute-start | bytes 884744 | tf_op jit(solution)/shard_map/ppermute | solution.py:100
  533.7 9.7 %collective-permute-start.14 = (bf16[2,48,768]{2,1,0:T(8,128)(2,1)S(1)}, bf16[2,48,768]{2,1,0:T(8,128)(2,1)S(1)}, u32[]{:S(2)}, u32[]{:S(2)}) collective-permute-start(bf16[2,48,768]{2,1,0:T(8,128)(2,1)S(1)} %fusion.166), channel_id=1, source_target_pairs={{0,16},{4,20},{8,24},{12,28},{16,0},{20,4},{24,8},{28,12},{1,17},{... | collective-permute-start | bytes 442376 | tf_op jit(solution)/shard_map/ppermute | solution.py:100
  537.6 27.2 %collective-permute-start.3 = (bf16[1,2,24,3200]{3,2,1,0:T(8,128)(2,1)}, bf16[1,2,24,3200]{3,2,1,0:T(8,128)(2,1)}, u32[]{:S(2)}, u32[]{:S(2)}) collective-permute-start(bf16[1,2,24,3200]{3,2,1,0:T(8,128)(2,1)} %get-tuple-element.531), channel_id=1, source_target_pairs={{0,8},{4,12},{8,0},{12,4},{16,24},{20,28},{24,16},{28,20},{1,9},{5... | collective-permute-start | bytes 921608 | tf_op jit(solution)/shard_map/ppermute | solution.py:100
  543.0 9.0 %collective-permute-start.9 = (bf16[2,48,768]{2,1,0:T(8,128)(2,1)S(1)}, bf16[2,48,768]{2,1,0:T(8,128)(2,1)S(1)}, u32[]{:S(2)}, u32[]{:S(2)}) collective-permute-start(bf16[2,48,768]{2,1,0:T(8,128)(2,1)S(1)} %fusion.164), channel_id=1, source_target_pairs={{0,16},{4,20},{8,24},{12,28},{16,0},{20,4},{24,8},{28,12},{1,17},{... | collective-permute-start | bytes 442376 | tf_op jit(solution)/shard_map/ppermute | solution.py:100
  565.8 10.5 %collective-permute-start.4 = (bf16[1,24,3200]{2,1,0:T(8,128)(2,1)S(1)}, bf16[1,24,3200]{2,1,0:T(8,128)(2,1)S(1)}, u32[]{:S(2)}, u32[]{:S(2)}) collective-permute-start(bf16[1,24,3200]{2,1,0:T(8,128)(2,1)S(1)} %fusion.162), channel_id=1, source_target_pairs={{0,16},{4,20},{8,24},{12,28},{16,0},{20,4},{24,8},{28,12},{1,17},{... | collective-permute-start | bytes 460808 | tf_op jit(solution)/shard_map/ppermute | solution.py:100
  566.9 18.4 %copy-start.1 = (bf16[1536,768]{1,0:T(8,128)(2,1)S(1)}, bf16[1536,768]{1,0:T(8,128)(2,1)}, u32[]{:S(2)}) copy-start(bf16[1536,768]{1,0:T(8,128)(2,1)} %param.38) | copy-start | bytes 7077892
  (148 other events, 677.3 us)
where the time goes:
time: 594 us; the launch traced here: 586 us
  matrix products  140 us (24%)
  local copies, waits for them, and re-layouts  119 us (20%)
  waiting for transfers between devices  105 us (18%)
  blocking collectives  95.5 us (16%)
  other arithmetic  73.8 us (12%)
  starting transfers between devices  49.7 us (8%)
    psum x1, blocking collectives, local(): lax.psum((g_bmix, g_bvalue, g_bout, g_qscale, g_qshift, g_gain, g_lnbias,...  42.2 us
    ppermute x15, waiting for transfers between devices, exchange(): return lax.ppermute(part, axis, [(i, i ^ 1 << bit) for i in range(size)])  38.3 us
    dot_general x3, matrix products, ema_core(): inner = jnp.einsum('dts,ndbs->ndbt', toeplitz, blocks, precision=highest)  28.2 us
    convert_element_type x15, other arithmetic, pick(): (half.astype(jnp.float32) + other.astype(jnp.float32)).astype(jnp.bfloat16)  25.8 us
    all_to_all x1, waiting for transfers between devices, local(): lax.all_to_all(grad_masked, 'ch', split_axis=2, concat_axis=1, tiled=True)  24.8 us
    all_gather x3, blocking collectives, reduce_rows(): whole = lax.all_gather(total, 'tok', axis=1)  23.1 us
    all_to_all x1, waiting for transfers between devices, local(): lax.all_to_all(activ.astype(jnp.bfloat16), 'ch', split_axis=2, concat_axi...  21.6 us
    all_to_all x1, waiting for transfers between devices, local(): lax.all_to_all(from_rows(result.astype(jnp.bfloat16), nseq_count), 'ch',...  19.9 us
  transfers between devices with their start and end apart: 21, of which 8 were waited for; matrix products, arithmetic and copies ran while one was open for 39% of the time, Pallas kernels for 0%

commit v1 on v0

--- a/solution.py
+++ b/solution.py
@@ -338,8 +338,10 @@
     )
     summed = (g_mix_s, g_value_s, g_out_s, g_up_s, g_down_s) + ema_grads
     smalls = lax.psum(
-        (g_bmix, g_bvalue, g_bout, g_qscale, g_qshift, g_gain, g_lnbias, g_bup, g_bdown),
-        ("ch", "tok"),
+        lax.psum(
+            (g_bmix, g_bvalue, g_bout, g_qscale, g_qshift, g_gain, g_lnbias, g_bup, g_bdown), "tok"
+        ),
+        "ch",
     )
     return (
         output,

time: 594 us -> 616 us (1.037)
  other arithmetic: 73.8 us -> 87 us
  waiting for transfers between devices: 105 us -> 115 us
    ppermute x15, waiting for transfers between devices: 38.3 us -> 45.5 us  [exchange(): return lax.ppermute(part, axis, [(i, i ^ 1 << bit) for i in range(size)])]
    unnamed x306 -> x320, local copies, waits for them, and re-layouts: 19.4 us -> 19.4 us
  transfers between devices with their start and end apart: 21 -> 21, of which waited for: 8 -> 10; matrix products, arithmetic and copies ran while one was open for 39% -> 40% of each run, Pallas kernels for 0% -> 0%
where the time goes in v1:
time: 616 us; the launch traced here: 607 us
  matrix products  141 us (23%)
  local copies, waits for them, and re-layouts  122 us (20%)
  waiting for transfers between devices  115 us (19%)
  blocking collectives  93.6 us (15%)
  other arithmetic  87 us (14%)
  starting transfers between devices  45.2 us (7%)
    ppermute x15, waiting for transfers between devices, exchange(): return lax.ppermute(part, axis, [(i, i ^ 1 << bit) for i in range(size)])  45.5 us
    psum x1, blocking collectives, local(): lax.psum(lax.psum((g_bmix, g_bvalue, g_bout, g_qscale, g_qshift, g_gain,...  36.7 us
    dot_general x3, matrix products, ema_core(): inner = jnp.einsum('dts,ndbs->ndbt', toeplitz, blocks, precision=highest)  27.7 us
    convert_element_type x15, other arithmetic, pick(): (half.astype(jnp.float32) + other.astype(jnp.float32)).astype(jnp.bfloat16)  25.7 us
    all_to_all x1, waiting for transfers between devices, local(): lax.all_to_all(grad_masked, 'ch', split_axis=2, concat_axis=1, tiled=True)  23.5 us
    all_gather x3, blocking collectives, reduce_rows(): whole = lax.all_gather(total, 'tok', axis=1)  22.5 us
    all_to_all x1, waiting for transfers between devices, local(): lax.all_to_all(activ.astype(jnp.bfloat16), 'ch', split_axis=2, concat_axi...  21 us
    unnamed x320, local copies, waits for them, and re-layouts  19.4 us
  transfers between devices with their start and end apart: 21, of which 10 were waited for; matrix products, arithmetic and copies ran while one was open for 40% of the time, Pallas kernels for 0%

profile of v1, /device:TPU:0, one launch (start us, length us, event | category | flops | bytes accessed | tf_op | source)
XLA Modules:
  0.0 607.1 jit_solution(6634405016666726052)
XLA Ops:
  3.2 7.3 %all-to-all-start.1 = ((bf16[4,96,1024]{1,0,2:T(4,128)(2,1)}), bf16[4,96,1024]{1,0,2:T(4,128)(2,1)}, u32[]{:S(2)}, u32[]{:S(2)}) async-start(bf16[4,96,1024]{1,0,2:T(4,128)(2,1)} %copy.451), calls=%async_computation.1 | async-start | bytes 2097152 | tf_op jit(solution)/shard_map/all_to_all | solution.py:181
  35.1 7.6 %while.30 = (s32[]{:T(128)}, f32[4,96,16]{1,2,0:T(8,128)}, s32[]{:T(128)}, f32[4,96,16]{1,2,0:T(8,128)}, f32[4,4,96,16]{2,3,1,0:T(8,128)S(1)}, /*index=5*/s32[]{:T(128)}, s32[]{:T(128)}) while((s32[]{:T(128)}, f32[4,96,16]{1,2,0:T(8,128)}, s32[]{:T(128)}, f32[4,96,16]{1,2,0:T(8,128)}, f32[4,4,96,16]{2,3,1,0:T(8,128)S(1)}, ...), condition=%wide.region_1.2_spmd.clone, body=%wide.region_0.1_spmd.clone.sunk | while | flops 24580 | bytes 92273 | solution.py:25
  65.5 10.1 %bitcast_add_fusion.3 = f32[4,96,8,128]{3,2,0,1:T(8,128)} fusion(f32[96,4,8,128]{3,2,1,0:T(8,128)S(1)} %fusion.92, f32[96,128,128,1]{2,0,1,3:T(8,128)} %fusion.29, bf16[4,96,8,128]{3,2,1,0:T(8,128)(2,1)S(1)} %bitcast.447), kind=kOutput, calls=%fused_computation.130 | convolution fusion | flops 604372992 | bytes 10223616 | tf_op jit(solution)/shard_map/dts,ndbs->ndbt/dot_general | solution.py:49
  96.8 21.0 %all-to-all-done = bf16[4,96,1024]{1,0,2:T(4,128)(2,1)} async-done(((bf16[4,96,1024]{1,0,2:T(4,128)(2,1)}), bf16[4,96,1024]{1,0,2:T(4,128)(2,1)}, u32[]{:S(2)}, u32[]{:S(2)}) %all-to-all-start) | async-done | bytes 786464 | tf_op jit(solution)/shard_map/all_to_all | solution.py:182
  152.1 18.6 %all-to-all-done.2 = bf16[4,768,128]{2,0,1:T(4,128)(2,1)} async-done(((bf16[4,768,128]{2,0,1:T(4,128)(2,1)}), bf16[4,768,128]{2,0,1:T(4,128)(2,1)}, u32[]{:S(2)}, u32[]{:S(2)}) %all-to-all-start.2) | async-done | bytes 786464 | tf_op jit(solution)/shard_map/all_to_all | solution.py:233
  182.0 23.5 %all-to-all-done.3 = bf16[4,96,1024]{1,0,2:T(4,128)(2,1)} async-done(((bf16[4,96,1024]{1,0,2:T(4,128)(2,1)}), bf16[4,96,1024]{1,0,2:T(4,128)(2,1)}, u32[]{:S(2)}, u32[]{:S(2)}) %all-to-all-start.3) | async-done | bytes 786464 | tf_op jit(solution)/shard_map/all_to_all | solution.py:244
  240.2 6.7 %convolution_convert_fusion.5 = bf16[512,768]{1,0:T(8,128)(2,1)} fusion(bf16[768,3200]{1,0:T(8,128)(2,1)} %param.34, bf16[512,768]{1,0:T(8,128)(2,1)S(1)} %copy-done.46, bf16[512,1536]{1,0:T(8,128)(2,1)} %get-tuple-element.520, bf16[512,128]{1,0:T(8,128)(2,1)S(1)} %get-tuple-element.522, bf16[512,768]{1,0:T(8,128)(2,1)S(1)} %copy-done.47), kind=kOutput, calls=%fused_computation.158 | convolution fusion | flops 2530082816 | bytes 8978432 | tf_op jit(solution)/shard_map/dot_general | solution.py:304
  298.3 6.3 %all-to-all-start.4 = ((bf16[4,768,128]{2,0,1:T(4,128)(2,1)}), bf16[4,768,128]{2,0,1:T(4,128)(2,1)}, u32[]{:S(2)}, u32[]{:S(2)}) async-start(bf16[4,768,128]{2,0,1:T(4,128)(2,1)} %bitcast.467), calls=%async_computation.4 | async-start | bytes 1572864 | tf_op jit(solution)/shard_map/all_to_all | solution.py:306
  353.2 6.9 %all-gather.2 = f32[16,96,16]{1,2,0:T(8,128)} all-gather(f32[4,96,16]{1,2,0:T(8,128)} %copy.471), channel_id=4, replica_groups=mesh['ch'=8,'tok'=4] {'tok'}, dimensions={0}, use_global_device_ids=true | all-gather | bytes 122880 | tf_op jit(solution)/shard_map/all_gather | solution.py:12
  360.1 8.7 %while.31 = (s32[]{:T(128)}, f32[4,96,16]{1,2,0:T(8,128)}, s32[]{:T(128)}, f32[4,96,16]{1,2,0:T(8,128)}, f32[4,4,96,16]{2,3,1,0:T(8,128)}, /*index=5*/s32[]{:T(128)}, s32[]{:T(128)}, s32[]{:T(128)}, s32[]{:T(128)}) while((s32[]{:T(128)}, f32[4,96,16]{1,2,0:T(8,128)}, s32[]{:T(128)}, f32[4,96,16]{1,2,0:T(8,128)}, ...), condition=%wide.region_11.12_spmd.clone, body=%wide.region_10.11_spmd.clone.sunk | while | flops 24584 | bytes 92335 | solution.py:25
  370.4 7.1 %multiply_reduce_fusion = (f32[96,16]{1,0:T(8,128)}, f32[96,16]{1,0:T(8,128)}) fusion(f32[96,16]{1,0:T(8,128)} %copy-done.71, f32[1024]{0:T(1024)} %multiply_add_fusion.4, f32[96,16]{1,0:T(8,128)} %copy-done.68, f32[96,4,16]{2,1,0:T(4,128)} %copy.472, bf16[4,96,1024]{2,1,0:T(8,128)(2,1)S(1)} %copy-done.18), kind=kOutput, calls=%fused_computation.13 | convolution fusion | flops 86504448 | bytes 839680 | tf_op jit(solution)/shard_map/transpose(jvp(djs,nds->ndj))/dot_general | solution.py:74
  385.2 11.1 %add_bitcast_fusion = f32[4,96,8,128]{3,2,0,1:T(8,128)} fusion(f32[96,4,8,128]{3,2,1,0:T(8,128)S(1)} %fusion.95, f32[96,128,128,1]{2,0,1,3:T(8,128)} %fusion.29, f32[4,96,8,128]{3,2,0,1:T(8,128)S(1)} %copy-done.15), kind=kOutput, calls=%fused_computation.139 | convolution fusion | flops 604372992 | bytes 11010048 | tf_op jit(solution)/shard_map/transpose(jvp(dts,ndbs->ndbt))/dot_general | solution.py:49
  399.1 6.6 %bitcast_add_fusion.2 = f32[4,96,1024]{2,0,1:T(4,128)S(1)} fusion(f32[4,96,1024]{2,0,1:T(4,128)} %reshape.714, f32[4,96,1024]{2,0,1:T(4,128)} %reshape.713, f32[4,96,1024]{2,0,1:T(4,128)} %get-tuple-element.510, f32[96,4,16]{2,1,0:T(4,128)} %copy.472, f32[96,16]{1,0:T(8,128)} %copy-done.71, f32[1024]{0:T(1024)} %multiply_add_fusion.4, ...), kind=kOutput, calls=%fused_computation.123 | convolution fusion | flops 80216064 | bytes 6332800 | tf_op jit(solution)/shard_map/transpose(jvp(djs,nds->ndj))/dot_general | solution.py:74
  414.9 6.5 %convolution_bitcast_fusion = f32[96,128,128]{2,1,0:T(8,128)S(1)} fusion(f32[4,96,8,128]{3,2,0,1:T(8,128)} %reshape.712, bf16[4,96,8,128]{3,2,1,0:T(8,128)(2,1)S(1)} %bitcast.449), kind=kOutput, calls=%fused_computation.78 | convolution fusion | flops 603979776 | bytes 8650752 | tf_op jit(solution)/shard_map/transpose(jvp(dts,ndbs->ndbt))/dot_general | solution.py:49
  421.4 7.9 %fusion.2 = f32[96,128,1]{1,0,2:T(8,128)S(1)} fusion(f32[96,128,128]{2,1,0:T(8,128)S(1)} %convolution_bitcast_fusion, f32[128,128]{1,0:T(8,128)S(1)} %copy-done.78), kind=kOutput, calls=%fused_computation.7 | convolution fusion | flops 2418016256 | bytes 6406144 | tf_op jit(solution)/shard_map/transpose(jvp(dm,mts->dts))/dot_general | solution.py:47
  454.6 7.8 %collective-permute-done.11 = bf16[2,2,2,2,48,768]{5,4,0,1,3,2:T(8,128)(2,1)} collective-permute-done((bf16[2,2,2,2,48,768]{5,4,0,1,3,2:T(8,128)(2,1)}, bf16[2,2,2,2,48,768]{5,4,0,1,3,2:T(8,128)(2,1)}, u32[]{:S(2)}, u32[]{:S(2)}) %collective-permute-start.11) | collective-permute-done | bytes 1179680 | tf_op jit(solution)/shard_map/ppermute | solution.py:100
  469.7 19.0 %collective-permute-done.1 = bf16[1,2,2,2,24,3200]{5,4,1,3,2,0:T(8,128)(2,1)} collective-permute-done((bf16[1,2,2,2,24,3200]{5,4,1,3,2,0:T(8,128)(2,1)}, bf16[1,2,2,2,24,3200]{5,4,1,3,2,0:T(8,128)(2,1)}, u32[]{:S(2)}, u32[]{:S(2)}) %collective-permute-start.1) | collective-permute-done | bytes 1228832 | tf_op jit(solution)/shard_map/ppermute | solution.py:100
  492.8 16.0 %all-reduce.9 = (f32[96,16]{0,1:T(8,128)}, f32[96,16]{0,1:T(8,128)}, f32[96,16]{0,1:T(8,128)}, f32[96,16]{0,1:T(8,128)}, f32[96]{0:T(128)}, /*index=5*/f32[3200]...) all-reduce(f32[96,16]{0,1:T(8,128)S(1)} %copy-done.113, ...), channel_id=1, replica_groups=mesh['ch'=8,'tok'=4] {'tok'}, use_global_device_ids=true, to_apply=%region_23.24 | all-reduce | flops 16096 | bytes 128768 | tf_op jit(solution)/shard_map/psum | solution.py:336
  508.8 36.7 %all-reduce.8 = (f32[3200]{0:T(1024)}, f32[1536]{0:T(1024)}, f32[768]{0:T(1024)}, f32[2,128]{1,0:T(2,128)}, f32[2,128]{1,0:T(2,128)}, /*index=5*/f32[768]{0:T(10...) all-reduce(f32[3200]{0:T(1024)S(1)} %get-tuple-element.496, ...), channel_id=1, replica_groups=mesh['ch'=8,'tok'=4] {'ch'}, use_global_device_ids=true, to_apply=%region_32.33 | all-reduce | flops 9856 | bytes 78848 | tf_op jit(solution)/shard_map/psum | solution.py:340
  552.1 6.7 %collective-permute-done.13 = bf16[2,2,48,768]{3,2,0,1:T(8,128)(2,1)S(1)} collective-permute-done((bf16[2,2,48,768]{3,2,0,1:T(8,128)(2,1)S(1)}, bf16[2,2,48,768]{3,2,0,1:T(8,128)(2,1)S(1)}, u32[]{:S(2)}, u32[]{:S(2)}) %collective-permute-start.13) | collective-permute-done | bytes 294944 | tf_op jit(solution)/shard_map/ppermute | solution.py:100
  565.7 7.4 %all-gather.5 = bf16[2,192,768]{2,1,0:T(8,128)(2,1)S(1)} all-gather(bf16[2,48,768]{2,1,0:T(8,128)(2,1)S(1)} %fusion.144), channel_id=7, replica_groups=mesh['ch'=8,'tok'=4] {'tok'}, dimensions={1}, use_global_device_ids=true | all-gather | bytes 737280 | tf_op jit(solution)/shard_map/all_gather | solution.py:129
  573.1 7.7 %all-gather.4 = bf16[2,192,768]{2,1,0:T(8,128)(2,1)S(1)} all-gather(bf16[2,48,768]{2,1,0:T(8,128)(2,1)S(1)} %fusion.147), channel_id=6, replica_groups=mesh['ch'=8,'tok'=4] {'tok'}, dimensions={1}, use_global_device_ids=true | all-gather | bytes 737280 | tf_op jit(solution)/shard_map/all_gather | solution.py:129
  587.8 9.4 %collective-permute-done.4 = bf16[1,24,3200]{2,1,0:T(8,128)(2,1)S(1)} collective-permute-done((bf16[1,24,3200]{2,1,0:T(8,128)(2,1)S(1)}, bf16[1,24,3200]{2,1,0:T(8,128)(2,1)S(1)}, u32[]{:S(2)}, u32[]{:S(2)}) %collective-permute-start.4) | collective-permute-done | bytes 153632 | tf_op jit(solution)/shard_map/ppermute | solution.py:100
  598.1 7.5 %all-gather.3 = bf16[4,24,3200]{2,1,0:T(8,128)(2,1)S(1)} all-gather(bf16[1,24,3200]{2,1,0:T(8,128)(2,1)S(1)} %fusion.139), channel_id=5, replica_groups=mesh['ch'=8,'tok'=4] {'tok'}, dimensions={0}, use_global_device_ids=true | all-gather | bytes 768000 | tf_op jit(solution)/shard_map/all_gather | solution.py:129
  (537 shorter events, 346.3 us)
Async XLA Ops:
  0.7 135.2 %copy-start = (bf16[1536,768]{1,0:T(8,128)(2,1)S(1)}, bf16[1536,768]{1,0:T(8,128)(2,1)}, u32[]{:S(2)}) copy-start(bf16[1536,768]{1,0:T(8,128)(2,1)} %param.38) | copy-start | bytes 7077892
  3.2 82.1 %all-to-all-start.1 = ((bf16[4,96,1024]{1,0,2:T(4,128)(2,1)}), bf16[4,96,1024]{1,0,2:T(4,128)(2,1)}, u32[]{:S(2)}, u32[]{:S(2)}) async-start(bf16[4,96,1024]{1,0,2:T(4,128)(2,1)} %copy.451), calls=%async_computation.1 | async-start | bytes 2097152 | tf_op jit(solution)/shard_map/all_to_all | solution.py:181
  85.3 32.5 %all-to-all-start = ((bf16[4,96,1024]{1,0,2:T(4,128)(2,1)}), bf16[4,96,1024]{1,0,2:T(4,128)(2,1)}, u32[]{:S(2)}, u32[]{:S(2)}) async-start(bf16[4,96,1024]{1,0,2:T(4,128)(2,1)} %copy.447), calls=%async_computation | async-start | bytes 2097152 | tf_op jit(solution)/shard_map/all_to_all | solution.py:182
  146.3 24.4 %all-to-all-start.2 = ((bf16[4,768,128]{2,0,1:T(4,128)(2,1)}), bf16[4,768,128]{2,0,1:T(4,128)(2,1)}, u32[]{:S(2)}, u32[]{:S(2)}) async-start(bf16[4,768,128]{2,0,1:T(4,128)(2,1)} %bitcast.468), calls=%async_computation.2 | async-start | bytes 1572864 | tf_op jit(solution)/shard_map/all_to_all | solution.py:233
  175.7 29.8 %all-to-all-start.3 = ((bf16[4,96,1024]{1,0,2:T(4,128)(2,1)}), bf16[4,96,1024]{1,0,2:T(4,128)(2,1)}, u32[]{:S(2)}, u32[]{:S(2)}) async-start(bf16[4,96,1024]{1,0,2:T(4,128)(2,1)} %copy.459), calls=%async_computation.3 | async-start | bytes 2097152 | tf_op jit(solution)/shard_map/all_to_all | solution.py:244
  266.4 31.9 %all-to-all-start.5 = ((bf16[4,768,128]{2,0,1:T(4,128)(2,1)}), bf16[4,768,128]{2,0,1:T(4,128)(2,1)}, u32[]{:S(2)}, u32[]{:S(2)}) async-start(bf16[4,768,128]{2,0,1:T(4,128)(2,1)} %bitcast.54), calls=%async_computation.5 | async-start | bytes 1572864 | tf_op jit(solution)/shard_map/all_to_all | solution.py:313
  286.3 143.1 %collective-permute-start.10 = (bf16[2,2,2,2,2,48,768]{6,5,0,1,3,2,4:T(8,128)(2,1)}, bf16[2,2,2,2,2,48,768]{6,5,0,1,3,2,4:T(8,128)(2,1)}, u32[]{:S(2)}, u32[]{:S(2)}) collective-permute-start(bf16[2,2,2,2,2,48,768]{6,5,0,1,3,2,4:T(8,128)(2,1)} %copy_bitcast_fusion.1), channel_id=1, source_target_pairs={{0,1},{1,0},{2,3},{3,2},{4,5},{5,4},{6,7},{7,6},{8,9},{9,8},{10,11... | collective-permute-start | bytes 7077896 | tf_op jit(solution)/shard_map/ppermute | solution.py:100
  288.0 146.0 %collective-permute-start.5 = (bf16[2,2,2,2,2,48,768]{6,5,0,1,4,2,3:T(8,128)(2,1)}, bf16[2,2,2,2,2,48,768]{6,5,0,1,4,2,3:T(8,128)(2,1)}, u32[]{:S(2)}, u32[]{:S(2)}) collective-permute-start(bf16[2,2,2,2,2,48,768]{6,5,0,1,4,2,3:T(8,128)(2,1)} %copy_bitcast_fusion.2), channel_id=1, source_target_pairs={{0,1},{1,0},{2,3},{3,2},{4,5},{5,4},{6,7},{7,6},{8,9},{9,8},{10,11... | collective-permute-start | bytes 7077896 | tf_op jit(solution)/shard_map/ppermute | solution.py:100
  292.3 145.8 %collective-permute-start = (bf16[1,2,2,2,2,24,3200]{6,5,1,3,2,4,0:T(8,128)(2,1)}, bf16[1,2,2,2,2,24,3200]{6,5,1,3,2,4,0:T(8,128)(2,1)}, u32[]{:S(2)}, u32[]{:S(2)}) collective-permute-start(bf16[1,2,2,2,2,24,3200]{6,5,1,3,2,4,0:T(8,128)(2,1)} %copy_bitcast_fusion), channel_id=1, source_target_pairs={{0,1},{1,0},{2,3},{3,2},{4,5},{5,4},{6,7},{7,6},{8,9},{9,8},{10,11... | collective-permute-start | bytes 7372808 | tf_op jit(solution)/shard_map/ppermute | solution.py:100
  298.3 26.7 %all-to-all-start.4 = ((bf16[4,768,128]{2,0,1:T(4,128)(2,1)}), bf16[4,768,128]{2,0,1:T(4,128)(2,1)}, u32[]{:S(2)}, u32[]{:S(2)}) async-start(bf16[4,768,128]{2,0,1:T(4,128)(2,1)} %bitcast.467), calls=%async_computation.4 | async-start | bytes 1572864 | tf_op jit(solution)/shard_map/all_to_all | solution.py:306
  433.3 29.1 %collective-permute-start.11 = (bf16[2,2,2,2,48,768]{5,4,0,1,3,2:T(8,128)(2,1)}, bf16[2,2,2,2,48,768]{5,4,0,1,3,2:T(8,128)(2,1)}, u32[]{:S(2)}, u32[]{:S(2)}) collective-permute-start(bf16[2,2,2,2,48,768]{5,4,0,1,3,2:T(8,128)(2,1)} %get-tuple-element.538), channel_id=1, source_target_pairs={{0,2},{1,3},{2,0},{3,1},{4,6},{5,7},{6,4},{7,5},{8,10},{9,11},{10,... | collective-permute-start | bytes 3538952 | tf_op jit(solution)/shard_map/ppermute | solution.py:100
  436.7 30.3 %collective-permute-start.6 = (bf16[2,2,2,2,48,768]{5,4,3,2,1,0:T(8,128)(2,1)}, bf16[2,2,2,2,48,768]{5,4,3,2,1,0:T(8,128)(2,1)}, u32[]{:S(2)}, u32[]{:S(2)}) collective-permute-start(bf16[2,2,2,2,48,768]{5,4,3,2,1,0:T(8,128)(2,1)} %fusion.36), channel_id=1, source_target_pairs={{0,4},{4,0},{8,12},{12,8},{16,20},{20,16},{24,28},{28,24},{1,5},{5... | collective-permute-start | bytes 3538952 | tf_op jit(solution)/shard_map/ppermute | solution.py:100
  441.9 46.8 %collective-permute-start.1 = (bf16[1,2,2,2,24,3200]{5,4,1,3,2,0:T(8,128)(2,1)}, bf16[1,2,2,2,24,3200]{5,4,1,3,2,0:T(8,128)(2,1)}, u32[]{:S(2)}, u32[]{:S(2)}) collective-permute-start(bf16[1,2,2,2,24,3200]{5,4,1,3,2,0:T(8,128)(2,1)} %get-tuple-element.534), channel_id=1, source_target_pairs={{0,2},{1,3},{2,0},{3,1},{4,6},{5,7},{6,4},{7,5},{8,10},{9,11},{10,... | collective-permute-start | bytes 3686408 | tf_op jit(solution)/shard_map/ppermute | solution.py:100
  464.8 24.0 %copy-start.34 = (bf16[1,2,2,2,24,3200]{5,4,1,3,2,0:T(8,128)(2,1)S(1)}, bf16[1,2,2,2,24,3200]{5,4,1,3,2,0:T(8,128)(2,1)}, u32[]{:S(2)}) copy-start(bf16[1,2,2,2,24,3200]{5,4,1,3,2,0:T(8,128)(2,1)} %get-tuple-element.533) | copy-start | bytes 3686404
  465.6 79.8 %collective-permute-start.12 = (bf16[2,2,2,48,768]{4,3,0,2,1:T(8,128)(2,1)}, bf16[2,2,2,48,768]{4,3,0,2,1:T(8,128)(2,1)}, u32[]{:S(2)}, u32[]{:S(2)}) collective-permute-start(bf16[2,2,2,48,768]{4,3,0,2,1:T(8,128)(2,1)} %copy.509), channel_id=1, source_target_pairs={{0,4},{4,0},{8,12},{12,8},{16,20},{20,16},{24,28},{28,24},{1,5},{5... | collective-permute-start | bytes 1769480 | tf_op jit(solution)/shard_map/ppermute | solution.py:100
  469.0 78.9 %collective-permute-start.7 = (bf16[2,2,2,48,768]{4,3,2,1,0:T(8,128)(2,1)}, bf16[2,2,2,48,768]{4,3,2,1,0:T(8,128)(2,1)}, u32[]{:S(2)}, u32[]{:S(2)}) collective-permute-start(bf16[2,2,2,48,768]{4,3,2,1,0:T(8,128)(2,1)} %fusion.116), channel_id=1, source_target_pairs={{0,2},{1,3},{2,0},{3,1},{4,6},{5,7},{6,4},{7,5},{8,10},{9,11},{10,... | collective-permute-start | bytes 1769480 | tf_op jit(solution)/shard_map/ppermute | solution.py:100
  490.5 55.0 %copy-start.50 = (bf16[2,2,2,1,48,768]{5,4,0,1,3,2:T(8,128)(2,1)S(1)}, bf16[2,2,2,1,48,768]{5,4,0,1,3,2:T(8,128)(2,1)}, u32[]{:S(2)}) copy-start(bf16[2,2,2,1,48,768]{5,4,0,1,3,2:T(8,128)(2,1)} %get-tuple-element.535) | copy-start | bytes 1769476
  491.4 67.5 %collective-permute-start.2 = (bf16[1,2,2,24,3200]{4,3,2,1,0:T(8,128)(2,1)}, bf16[1,2,2,24,3200]{4,3,2,1,0:T(8,128)(2,1)}, u32[]{:S(2)}, u32[]{:S(2)}) collective-permute-start(bf16[1,2,2,24,3200]{4,3,2,1,0:T(8,128)(2,1)} %copy.493), channel_id=1, source_target_pairs={{0,4},{4,0},{8,12},{12,8},{16,20},{20,16},{24,28},{28,24},{1,5},{5... | collective-permute-start | bytes 1843208 | tf_op jit(solution)/shard_map/ppermute | solution.py:100
  546.7 12.1 %collective-permute-start.13 = (bf16[2,2,48,768]{3,2,0,1:T(8,128)(2,1)S(1)}, bf16[2,2,48,768]{3,2,0,1:T(8,128)(2,1)S(1)}, u32[]{:S(2)}, u32[]{:S(2)}) collective-permute-start(bf16[2,2,48,768]{3,2,0,1:T(8,128)(2,1)S(1)} %get-tuple-element.542), channel_id=1, source_target_pairs={{0,8},{4,12},{8,0},{12,4},{16,24},{20,28},{24,16},{28,20},{1,9},{5... | collective-permute-start | bytes 884744 | tf_op jit(solution)/shard_map/ppermute | solution.py:100
  549.0 12.9 %collective-permute-start.8 = (bf16[2,2,48,768]{3,2,1,0:T(8,128)(2,1)S(1)}, bf16[2,2,48,768]{3,2,1,0:T(8,128)(2,1)S(1)}, u32[]{:S(2)}, u32[]{:S(2)}) collective-permute-start(bf16[2,2,48,768]{3,2,1,0:T(8,128)(2,1)S(1)} %fusion.141), channel_id=1, source_target_pairs={{0,8},{4,12},{8,0},{12,4},{16,24},{20,28},{24,16},{28,20},{1,9},{5... | collective-permute-start | bytes 884744 | tf_op jit(solution)/shard_map/ppermute | solution.py:100
  558.8 6.8 %collective-permute-start.14 = (bf16[2,48,768]{2,1,0:T(8,128)(2,1)S(1)}, bf16[2,48,768]{2,1,0:T(8,128)(2,1)S(1)}, u32[]{:S(2)}, u32[]{:S(2)}) collective-permute-start(bf16[2,48,768]{2,1,0:T(8,128)(2,1)S(1)} %fusion.166), channel_id=1, source_target_pairs={{0,16},{4,20},{8,24},{12,28},{16,0},{20,4},{24,8},{28,12},{1,17},{... | collective-permute-start | bytes 442376 | tf_op jit(solution)/shard_map/ppermute | solution.py:100
  561.0 24.9 %collective-permute-start.3 = (bf16[1,2,24,3200]{3,2,1,0:T(8,128)(2,1)}, bf16[1,2,24,3200]{3,2,1,0:T(8,128)(2,1)}, u32[]{:S(2)}, u32[]{:S(2)}) collective-permute-start(bf16[1,2,24,3200]{3,2,1,0:T(8,128)(2,1)} %get-tuple-element.540), channel_id=1, source_target_pairs={{0,8},{4,12},{8,0},{12,4},{16,24},{20,28},{24,16},{28,20},{1,9},{5... | collective-permute-start | bytes 921608 | tf_op jit(solution)/shard_map/ppermute | solution.py:100
  562.0 11.1 %collective-permute-start.9 = (bf16[2,48,768]{2,1,0:T(8,128)(2,1)S(1)}, bf16[2,48,768]{2,1,0:T(8,128)(2,1)S(1)}, u32[]{:S(2)}, u32[]{:S(2)}) collective-permute-start(bf16[2,48,768]{2,1,0:T(8,128)(2,1)S(1)} %fusion.164), channel_id=1, source_target_pairs={{0,16},{4,20},{8,24},{12,28},{16,0},{20,4},{24,8},{28,12},{1,17},{... | collective-permute-start | bytes 442376 | tf_op jit(solution)/shard_map/ppermute | solution.py:100
  586.8 10.3 %collective-permute-start.4 = (bf16[1,24,3200]{2,1,0:T(8,128)(2,1)S(1)}, bf16[1,24,3200]{2,1,0:T(8,128)(2,1)S(1)}, u32[]{:S(2)}, u32[]{:S(2)}) collective-permute-start(bf16[1,24,3200]{2,1,0:T(8,128)(2,1)S(1)} %fusion.162), channel_id=1, source_target_pairs={{0,16},{4,20},{8,24},{12,28},{16,0},{20,4},{24,8},{28,12},{1,17},{... | collective-permute-start | bytes 460808 | tf_op jit(solution)/shard_map/ppermute | solution.py:100
  (155 other events, 764.6 us)
